TPU v7x, 32 devices: a whole 2x2x4 slice. The times are simulated.
32 devices in a mesh: panel: 8 (over z, core), tm: 4 (over y, x).
Axes of the slice: x: 2, y: 2, z: 4, core: 2. Of those that a mesh axis runs over, the one named last changes fastest.
Arguments:
- pressures: bfloat16 [49152, 3072], P('panel', 'tm'), may hold values from -60 to 60
- sketch: bfloat16 [49152, 128], P(('panel', 'tm')), may hold values from -6 to 6
Outputs:
- basis_rows: bfloat16 [3072, 128], P('tm')
- image: float32 [49152, 128], P(('panel', 'tm'))
All inputs are finite; a program needn't handle non-finite values.
Results may differ from a plain program's by a relative error of at most 0.0029.
Values may be sent and summed in bfloat16 or wider, within the bound.
A program may use at most 64 MiB of HBM per device.

v0:
```python
import jax
import jax.numpy as jnp
from jax import lax
from jax.sharding import PartitionSpec as P


def gram_of(rows_block):
    return lax.dot_general(
        rows_block,
        rows_block,
        (((0,), (0,)), ((), ())),
        precision=lax.Precision.HIGHEST,
        preferred_element_type=jnp.float32,
    )


def orthonormal(rows_block, gram_matrix):
    lower_factor = jnp.linalg.cholesky(gram_matrix)
    solved = jax.scipy.linalg.solve_triangular(lower_factor, rows_block.T, lower=True)
    return solved.T.astype(jnp.bfloat16)


def on_device(pressures, sketch):
    partial_y = lax.dot_general(
        pressures,
        lax.all_gather(sketch, "tm", axis=0, tiled=True),
        (((0,), (0,)), ((), ())),
        preferred_element_type=jnp.float32,
    )
    y_rows = lax.psum(partial_y, "panel")
    gram_matrix = lax.psum(gram_of(y_rows), "tm")
    basis_rows = orthonormal(y_rows, gram_matrix)
    own_rows = pressures.shape[0] // lax.axis_size("tm")
    full_image = lax.psum(jnp.dot(pressures, basis_rows, preferred_element_type=jnp.float32), "tm")
    image = lax.dynamic_slice_in_dim(full_image, lax.axis_index("tm") * own_rows, own_rows, 0)
    return (basis_rows, image)


def solution(mesh):
    return jax.shard_map(
        on_device,
        mesh=mesh,
        in_specs=(P("panel", "tm"), P(("panel", "tm"), None)),
        out_specs=(P("tm", None), P(("panel", "tm"), None)),
        check_vma=False,
    )
```

profile of v0, /device:TPU:0, one launch (start us, length us, event | category | flops | bytes accessed | tf_op | source)
XLA Modules:
  0.0 281.9 jit_solution(17793500576031440329)
XLA Ops:
  7.2 0.0 all-gather.2.cloned.1.call-start
  7.2 0.7 all-gather.2.cloned.1.call-update
  7.9 0.0 all-reduce.4.cloned.1.call-start
  7.9 35.6 %all-gather.2.cloned.1.call-done = bf16[6144,128]{1,0:T(8,128)(2,1)} async-done(((bf16[1536,128]{1,0:T(8,128)(2,1)}), bf16[6144,128]{1,0:T(8,128)(2,1)}) %all-gather.2.cloned.1.call-update) | async-done | bytes 1572880 | tf_op jit(solution)/shard_map/all_gather | solution.py:26
  43.5 7.5 %fusion.3 = f32[768,128]{1,0:T(8,128)} fusion(bf16[6144,768]{1,0:T(8,128)(2,1)} %param.2, bf16[6144,128]{1,0:T(8,128)(2,1)} %all-gather.2.cloned.1.call-done), kind=kOutput, calls=%fused_computation.12 | convolution fusion | flops 1207959552 | bytes 11403264 | tf_op jit(solution)/shard_map/dot_general | solution.py:24
  51.0 0.0 all-reduce.4.cloned.1.call-update
  51.0 0.0 all-reduce.6.cloned.1.call-start
  51.1 55.5 %all-reduce.4.cloned.1.call-done = f32[768,128]{1,0:T(8,128)} async-done(((f32[768,128]{1,0:T(8,128)}), f32[768,128]{1,0:T(8,128)}) %all-reduce.4.cloned.1.call-update) | async-done | bytes 393232 | tf_op jit(solution)/shard_map/psum | solution.py:30
  106.6 2.5 fusion.4
  109.2 0.0 all-reduce.6.cloned.1.call-update
  109.2 0.2 all-reduce.8.cloned.1.call-start
  109.4 41.4 %all-reduce.6.cloned.1.call-done = f32[128,128]{0,1:T(8,128)} async-done(((f32[128,128]{0,1:T(8,128)}), f32[128,128]{0,1:T(8,128)}) %all-reduce.6.cloned.1.call-update) | async-done | bytes 65552 | tf_op jit(solution)/shard_map/psum | solution.py:31
  150.8 0.9 copy.5
  151.7 0.9 fusion.2
  152.6 11.7 %cholesky.16 = f32[128,128]{1,0:T(8,128)S(1)} custom-call(f32[128,128]{1,0:T(8,128)S(1)} %fusion.2), custom_call_target="Cholesky" | custom-call | tf_op jit(solution)/shard_map/jit(cholesky)/cholesky | solution.py:18
  164.4 0.6 compare_reduce_fusion
  165.0 0.7 fusion
  165.7 9.8 %custom-call.7 = f32[1,128,128]{1,2,0:T(8,128)S(1)} custom-call(f32[1,128,128]{2,1,0:T(8,128)S(1)} %fusion), custom_call_target="InvertDiagBlocksLowerTriangular" | custom-call | tf_op jit(solution)/shard_map/jit(_solve_triangular)/triangular_solve | solution.py:19
  175.5 1.5 convolution_convert_fusion
  176.9 0.0 copy-start
  176.9 8.7 %convolution_bitcast_fusion = f32[6144,128]{0,1:T(8,128)} fusion(bf16[768,128]{1,0:T(8,128)(2,1)S(1)} %convolution_convert_fusion, bf16[6144,768]{1,0:T(8,128)(2,1)} %param.2), kind=kOutput, calls=%fused_computation | convolution fusion | flops 1207959552 | bytes 12779520 | tf_op jit(solution)/shard_map/dot_general | solution.py:34
  185.6 0.0 copy-done
  185.6 0.0 all-reduce.8.cloned.1.call-update
  185.6 87.4 %all-reduce.8.cloned.1.call-done = f32[6144,128]{0,1:T(8,128)} async-done(((f32[6144,128]{0,1:T(8,128)}), f32[6144,128]{0,1:T(8,128)}) %all-reduce.8.cloned.1.call-update) | async-done | bytes 3145744 | tf_op jit(solution)/shard_map/psum | solution.py:34
  273.0 1.2 constant_dynamic-slice_fusion
  274.2 1.1 copy.6
  (1 shorter events, 0.0 us)
Async XLA Ops:
  7.2 36.4 %all-gather.2.cloned.1.call-start = ((), (), s32[]{:S(2)}) async-start(), calls=%async_computation | async-start | bytes 1966080 | tf_op jit(solution)/shard_map/all_gather | solution.py:26
  7.9 98.7 %all-reduce.4.cloned.1.call-start = ((), (), s32[]{:S(2)}) async-start(), calls=%async_computation.1 | async-start | bytes 786432 | tf_op jit(solution)/shard_map/psum | solution.py:30
  51.0 99.8 %all-reduce.6.cloned.1.call-start = ((), (), s32[]{:S(2)}) async-start(), calls=%async_computation.2 | async-start | bytes 131072 | tf_op jit(solution)/shard_map/psum | solution.py:31
  109.2 163.8 %all-reduce.8.cloned.1.call-start = ((), (), s32[]{:S(2)}) async-start(), calls=%async_computation.3 | async-start | bytes 6291456 | tf_op jit(solution)/shard_map/psum | solution.py:34
  176.9 8.7 %copy-start = (bf16[768,128]{1,0:T(8,128)(2,1)}, bf16[768,128]{1,0:T(8,128)(2,1)S(1)}, u32[]{:S(2)}) copy-start(bf16[768,128]{1,0:T(8,128)(2,1)S(1)} %convolution_convert_fusion) | copy-start | bytes 589828
Sparse Core Ops, SparseCore 0:
  9.8 33.6 all-gather.1
  51.2 55.4 all-reduce.3
  110.3 40.4 all-reduce.5
  185.8 87.1 all-reduce.7
where the time goes:
time: 282 us
  waiting for transfers between devices  221 us (78%)
  other arithmetic  23.7 us (8%)
  matrix products  20.1 us (7%)
  between operations  13.8 us (5%)
  local copies, waits for them, and re-layouts  3.27 us (1%)
    psum x1, waiting for transfers between devices, on_device(): lax.psum(jnp.dot(pressures, basis_rows, preferred_element_type=jnp.float3...  87.4 us
    psum x1, waiting for transfers between devices, on_device(): y_rows = lax.psum(partial_y, 'panel')  55.5 us
    psum x1, waiting for transfers between devices, on_device(): gram_matrix = lax.psum(gram_of(y_rows), 'tm')  41.4 us
    all_gather x1, waiting for transfers between devices, on_device(): lax.all_gather(sketch, 'tm', axis=0, tiled=True)  35.6 us
    another operation x3, other arithmetic, orthonormal(): lower_factor = jnp.linalg.cholesky(gram_matrix)  12.4 us
    another operation x2, other arithmetic, orthonormal(): jax.scipy.linalg.solve_triangular(lower_factor, rows_block.T, lower=True)  10.5 us
    dot_general x1, matrix products, on_device(): jnp.dot(pressures, basis_rows, preferred_element_type=jnp.float32)  8.66 us
    dot_general x1, matrix products, on_device(): lax.dot_general(pressures, lax.all_gather(sketch, 'tm', axis=0, tiled=Tru...  7.47 us
  transfers between devices with their start and end apart: 4, of which 4 were waited for; matrix products, arithmetic and copies ran while one was open for 0% of the time, Pallas kernels for 0%

commit v1 on v0

v1 whole, which is shorter than its diff:
```python
import functools

import jax
import jax.numpy as jnp
from jax import lax
from jax.experimental import pallas as pl
from jax.experimental.pallas import tpu as pltpu
from jax.sharding import PartitionSpec as P

MESH = pl.DeviceIdType.MESH
F32 = jnp.float32
BF16 = jnp.bfloat16
HIGHEST = lax.Precision.HIGHEST


def flipped(index, offset):
    bit = 1
    while bit <= offset:
        if offset & bit:
            index = index + bit - 2 * bit * lax.rem(lax.div(index, bit), 2)
        bit *= 2
    return index


def inverse_factor(aug, linv):
    k = linv.shape[0]
    sub = lax.broadcasted_iota(jnp.int32, (8, 2 * k), 0)
    for base in range(0, k, 8):
        block = aug[base : base + 8, :]
        s = {}
        for j in range(8):
            column = jnp.broadcast_to(block[:, base + j : base + j + 1], (8, k))
            for i in range(j, 8):
                s[i, j] = jnp.broadcast_to(column[i : i + 1, :], (8, k))
        rows = [jnp.broadcast_to(block[i : i + 1, :], (8, 2 * k)) for i in range(8)]
        recip = []
        for j in range(8):
            recip.append(1.0 / s[j, j])
            for i in range(j + 1, 8):
                m = s[i, j] * recip[j]
                for l in range(j + 1, i + 1):
                    s[i, l] = s[i, l] - m * s[l, j]
                rows[i] = rows[i] - jnp.concatenate([m, m], axis=1) * rows[j]
        done = rows[0]
        scale = recip[0]
        root = lax.rsqrt(s[0, 0])
        for j in range(1, 8):
            done = jnp.where(sub == j, rows[j], done)
            scale = jnp.where(sub[:, :k] == j, recip[j], scale)
            root = jnp.where(sub[:, :k] == j, lax.rsqrt(s[j, j]), root)
        linv[base : base + 8, :] = done[:, k:] * root
        if base + 8 < k:
            scaled = (done[:, :k] * scale).T[base + 8 :, :]
            aug[base + 8 :, :] = aug[base + 8 :, :] - jnp.dot(
                scaled, done, precision=HIGHEST, preferred_element_type=F32
            )


def kernel(
    n_panel, n_tm, p_hbm, s_hbm, basis_ref, image_ref,
    p_all, s_all, yt, y_full, core_in, z_in, g_own, g_in, aug, linv, basis, out_part, in_part, image,
    load_sem, s_load, s_send, s_recv, c_send, c_recv, z_send, z_recv, a_send, a_recv,
    b_send, b_recv, g_send, g_recv, o_send, o_recv, store_sem,
):
    panel, tm = lax.axis_index("panel"), lax.axis_index("tm")
    z, core = lax.div(panel, 2), lax.rem(panel, 2)
    n_z = n_panel // 2
    own = s_hbm.shape[0]
    k = s_hbm.shape[1]
    piece = k // n_panel
    half = k // 2

    def tm_partner(o):
        return (panel, flipped(tm, o))

    def z_partner(o):
        return (2 * flipped(z, o) + core, tm)

    other = (2 * z + 1 - core, tm)
    partners = [tm_partner(o) for o in range(1, n_tm)] + [z_partner(o) for o in range(1, n_z)] + [other]

    loads = []
    for o in range(n_tm):
        start = pl.multiple_of(flipped(tm, o) * own, own)
        load = pltpu.make_async_copy(p_hbm.at[pl.ds(start, own), :], p_all.at[o], load_sem.at[o])
        load.start()
        loads.append(load)
    own_load = pltpu.make_async_copy(s_hbm, s_all.at[0], s_load)
    own_load.start()

    barrier = pltpu.get_barrier_semaphore()
    for where in partners:
        pl.semaphore_signal(barrier, inc=1, device_id=where, device_id_type=MESH)
    pl.semaphore_wait(barrier, len(partners))

    def remote(src, dst, send, recv, where):
        copy = pltpu.make_async_remote_copy(
            src_ref=src, dst_ref=dst, send_sem=send, recv_sem=recv, device_id=where, device_id_type=MESH
        )
        copy.start()
        return copy

    sent = [
        remote(s_hbm, s_all.at[o], s_send.at[o], s_recv.at[o], tm_partner(o)) for o in range(1, n_tm)
    ]

    for o in range(n_tm):
        if o == 0:
            own_load.wait()
        else:
            sent[o - 1].wait_recv()
        loads[o].wait()
        product = lax.dot_general(
            s_all[o], p_all[o], (((0,), (0,)), ((), ())), preferred_element_type=F32
        )
        if o == 0:
            yt[...] = product
        else:
            yt[...] += product

    mine = pl.multiple_of(core * half, half)
    theirs = pl.multiple_of((1 - core) * half, half)
    copy = remote(yt.at[pl.ds(theirs, half), :], core_in, c_send, c_recv, other)
    copy.wait()
    yt[pl.ds(mine, half), :] += core_in[...]
    at = pl.multiple_of(mine + z * piece, piece)
    copies = []
    for o in range(1, n_z):
        there = pl.multiple_of(mine + flipped(z, o) * piece, piece)
        copies.append(remote(yt.at[pl.ds(there, piece), :], z_in.at[o], z_send.at[o], z_recv.at[o], z_partner(o)))
    total = yt[pl.ds(at, piece), :]
    for o in range(1, n_z):
        copies[o - 1].wait()
        total = total + z_in[o]
    y_full[pl.ds(at, piece), :] = total
    gathered = y_full.at[pl.ds(at, piece), :]
    copies = [
        remote(gathered, gathered, a_send.at[o], a_recv.at[o], z_partner(o)) for o in range(1, n_z)
    ]
    for copy in copies:
        copy.wait()
    gathered = y_full.at[pl.ds(mine, half), :]
    remote(gathered, gathered, b_send, b_recv, other).wait()

    rows = y_full[...]
    g_own[...] = lax.dot_general(
        rows, rows, (((1,), (1,)), ((), ())), precision=HIGHEST, preferred_element_type=F32
    )
    copies = [
        remote(g_own, g_in.at[o], g_send.at[o], g_recv.at[o], tm_partner(o)) for o in range(1, n_tm)
    ]
    gram = g_own[...]
    for o in range(1, n_tm):
        copies[o - 1].wait()
        gram = gram + g_in[o]
    aug[:, :k] = gram
    aug[:, k:] = (
        lax.broadcasted_iota(jnp.int32, (k, k), 0) == lax.broadcasted_iota(jnp.int32, (k, k), 1)
    ).astype(F32)
    inverse_factor(aug, linv)
    basis_t = jnp.dot(linv[...], y_full[...], precision=HIGHEST, preferred_element_type=F32)
    basis[...] = basis_t.T.astype(BF16)
    basis_store = pltpu.make_async_copy(basis, basis_ref, store_sem.at[0])
    basis_store.start()

    copies = []
    for o in range(n_tm - 1, 0, -1):
        out_part[o] = jnp.dot(p_all[o], basis[...], preferred_element_type=F32).astype(BF16)
        copies.append(remote(out_part.at[o], in_part.at[o], o_send.at[o], o_recv.at[o], tm_partner(o)))
    image[...] = jnp.dot(p_all[0], basis[...], preferred_element_type=F32)
    for o, copy in zip(range(n_tm - 1, 0, -1), copies):
        copy.wait()
        image[...] += in_part[o].astype(F32)
    store = pltpu.make_async_copy(image, image_ref, store_sem.at[1])
    store.start()
    for copy in sent:
        copy.wait_send()
    basis_store.wait()
    store.wait()


def on_device(n_panel, n_tm, pressures, sketch):
    own, k = sketch.shape
    nt = pressures.shape[1]
    n_z = n_panel // 2
    dma = pltpu.SemaphoreType.DMA
    return pl.pallas_call(
        functools.partial(kernel, n_panel, n_tm),
        out_shape=(jax.ShapeDtypeStruct((nt, k), BF16), jax.ShapeDtypeStruct((own, k), F32)),
        in_specs=[pl.BlockSpec(memory_space=pl.ANY)] * 2,
        out_specs=(pl.BlockSpec(memory_space=pl.ANY),) * 2,
        scratch_shapes=[
            pltpu.VMEM((n_tm, own, nt), BF16),
            pltpu.VMEM((n_tm, own, k), BF16),
            pltpu.VMEM((k, nt), F32),
            pltpu.VMEM((k, nt), F32),
            pltpu.VMEM((k // 2, nt), F32),
            pltpu.VMEM((n_z, k // n_panel, nt), F32),
            pltpu.VMEM((k, k), F32),
            pltpu.VMEM((n_tm, k, k), F32),
            pltpu.VMEM((k, 2 * k), F32),
            pltpu.VMEM((k, k), F32),
            pltpu.VMEM((nt, k), BF16),
            pltpu.VMEM((n_tm, own, k), BF16),
            pltpu.VMEM((n_tm, own, k), BF16),
            pltpu.VMEM((own, k), F32),
            dma((n_tm,)), dma, dma((n_tm,)), dma((n_tm,)),
            dma, dma, dma((n_z,)), dma((n_z,)), dma((n_z,)), dma((n_z,)),
            dma, dma, dma((n_tm,)), dma((n_tm,)), dma((n_tm,)), dma((n_tm,)), dma((2,)),
        ],
        compiler_params=pltpu.CompilerParams(
            collective_id=0, has_side_effects=True, vmem_limit_bytes=48 * 1024 * 1024
        ),
        cost_estimate=pl.CostEstimate(
            flops=4 * pressures.shape[0] * nt * k, bytes_accessed=2 * pressures.size, transcendentals=0
        ),
    )(pressures, sketch)


def solution(mesh):
    return jax.shard_map(
        functools.partial(on_device, mesh.shape["panel"], mesh.shape["tm"]),
        mesh=mesh,
        in_specs=(P("panel", "tm"), P(("panel", "tm"), None)),
        out_specs=(P("tm", None), P(("panel", "tm"), None)),
        check_vma=False,
    )
```

time: 282 us -> 78.9 us (0.28)
  waiting for transfers between devices: 221 us -> 0 us
  Pallas kernels: 0 us -> 75.6 us
  other arithmetic: 23.7 us -> 0 us
  matrix products: 20.1 us -> 0 us
  between operations: 13.8 us -> 0.65 us
    psum x3 -> x0, waiting for transfers between devices: 184 us -> none  [the longest x1 87.4 us: on_device(): lax.psum(jnp.dot(pressures, basis_rows, preferred_element_type=jnp.float3...]
    pallas_call x0 -> x1, Pallas kernels: none -> 75.6 us  [on_device(): pl.pallas_call(functools.partial(kernel, n_panel, n_tm), out_shape=(jax.S...]
    all_gather x1 -> x0, waiting for transfers between devices: 35.6 us -> none  [on_device(): lax.all_gather(sketch, 'tm', axis=0, tiled=True)]
    another operation x5 -> x0, other arithmetic: 22.9 us -> none  [the longest x3 12.4 us: orthonormal(): lower_factor = jnp.linalg.cholesky(gram_matrix)]
    dot_general x3 -> x0, matrix products: 18.7 us -> none  [the longest x1 8.66 us: on_device(): jnp.dot(pressures, basis_rows, preferred_element_type=jnp.float32)]
  transfers between devices with their start and end apart: 4 -> 0, of which waited for: 4 -> 0; matrix products, arithmetic and copies ran while one was open for 0% -> 0% of each run, Pallas kernels for 0% -> 0%
where the time goes in v1:
time: 78.9 us; the launch traced here: 78.8 us
  Pallas kernels  75.6 us (96%)
  local copies, waits for them, and re-layouts  2.55 us (3%)
    pallas_call x1, Pallas kernels, on_device(): pl.pallas_call(functools.partial(kernel, n_panel, n_tm), out_shape=(jax.S...  75.6 us
    unnamed x4, local copies, waits for them, and re-layouts  2.55 us

profile of v1, /device:TPU:0, one launch (start us, length us, event | category | flops | bytes accessed | tf_op | source)
XLA Modules:
  0.0 78.8 jit_solution(14655292245976333148)
XLA Ops:
  0.6 0.0 copy-start
  0.6 1.0 %copy-done = bf16[1536,128]{1,0:T(8,128)(2,1)S(1)} copy-done((bf16[1536,128]{1,0:T(8,128)(2,1)S(1)}, bf16[1536,128]{1,0:T(8,128)(2,1)}, u32[]{:S(2)}) %copy-start) | copy-done | bytes 393240
  1.6 75.6 %shard_map.41 = (bf16[768,128]{1,0:T(8,128)(2,1)S(1)}, f32[1536,128]{1,0:T(8,128)S(1)}) custom-call(bf16[6144,768]{1,0:T(8,128)(2,1)} %p_hbm.1, bf16[1536,128]{1,0:T(8,128)(2,1)S(1)} %copy-done), custom_call_target="tpu_custom_call" | custom-call | flops 2415919104 | bytes 9437184 | tf_op jit(solution)/shard_map/pallas_call | solution.py:187
  77.2 0.7 copy.6
  77.9 0.9 %copy.7 = f32[1536,128]{1,0:T(8,128)} copy(f32[1536,128]{1,0:T(8,128)S(1)} %get-tuple-element.5) | data formatting | bytes 1572864
Async XLA Ops:
  0.6 1.0 %copy-start = (bf16[1536,128]{1,0:T(8,128)(2,1)S(1)}, bf16[1536,128]{1,0:T(8,128)(2,1)}, u32[]{:S(2)}) copy-start(bf16[1536,128]{1,0:T(8,128)(2,1)} %s_hbm.1) | copy-start | bytes 1179652

commit v2 on v1

--- a/solution.py
+++ b/solution.py
@@ -100,15 +100,40 @@
         copy.start()
         return copy
 
-    sent = [
-        remote(s_hbm, s_all.at[o], s_send.at[o], s_recv.at[o], tm_partner(o)) for o in range(1, n_tm)
-    ]
+    low, high = pl.ds(0, own // 2), pl.ds(own // 2, own // 2)
+    parts = (low, high)
+
+    def send_sketch(o, h):
+        return remote(s_hbm.at[parts[h], :], s_all.at[o, parts[h], :], s_send.at[o, h], s_recv.at[o, h], tm_partner(o))
+
+    def forward_sketch(o, h):
+        rows = s_all.at[o, parts[h], :]
+        return remote(rows, s_all.at[3, parts[h], :], s_send.at[3, h], s_recv.at[3, h], tm_partner(3 - o))
+
+    arrivals = {}
+    if n_tm == 4:
+        for o, h in ((1, 0), (2, 1), (1, 1), (2, 0)):
+            arrivals[o, h] = send_sketch(o, h)
+    else:
+        for o in range(1, n_tm):
+            for h in range(2):
+                arrivals[o, h] = send_sketch(o, h)
 
     for o in range(n_tm):
         if o == 0:
             own_load.wait()
         else:
-            sent[o - 1].wait_recv()
+            if n_tm == 4 and o == 1:
+                arrivals[1, 0].wait_recv()
+                arrivals[3, 0] = forward_sketch(1, 0)
+                arrivals[2, 1].wait_recv()
+                arrivals[3, 1] = forward_sketch(2, 1)
+                arrivals[1, 1].wait_recv()
+            elif n_tm == 4 and o == 2:
+                arrivals[2, 0].wait_recv()
+            else:
+                arrivals[o, 0].wait_recv()
+                arrivals[o, 1].wait_recv()
         loads[o].wait()
         product = lax.dot_general(
             s_all[o], p_all[o], (((0,), (0,)), ((), ())), preferred_element_type=F32
@@ -163,17 +188,42 @@
     basis_store = pltpu.make_async_copy(basis, basis_ref, store_sem.at[0])
     basis_store.start()
 
-    copies = []
-    for o in range(n_tm - 1, 0, -1):
-        out_part[o] = jnp.dot(p_all[o], basis[...], preferred_element_type=F32).astype(BF16)
-        copies.append(remote(out_part.at[o], in_part.at[o], o_send.at[o], o_recv.at[o], tm_partner(o)))
-    image[...] = jnp.dot(p_all[0], basis[...], preferred_element_type=F32)
-    for o, copy in zip(range(n_tm - 1, 0, -1), copies):
-        copy.wait()
-        image[...] += in_part[o].astype(F32)
+    def partial(o, h):
+        return jnp.dot(p_all[o, parts[h], :], basis[...], preferred_element_type=F32)
+
+    def send_image(block, o, h):
+        out_part[o, parts[h], :] = block.astype(BF16)
+        return remote(out_part.at[o, parts[h], :], in_part.at[o, parts[h], :],
+                      o_send.at[o, h], o_recv.at[o, h], tm_partner(o))
+
+    copies = {}
+    if n_tm == 4:
+        diagonal = 3
+        for h in range(2):
+            out_part[diagonal, parts[h], :] = partial(diagonal, h).astype(BF16)
+            copies[diagonal, h] = remote(
+                out_part.at[diagonal, parts[h], :], in_part.at[diagonal, parts[h], :],
+                o_send.at[diagonal, h], o_recv.at[diagonal, h], tm_partner(1 + h),
+            )
+        for o, h in ((1, 0), (2, 1)):
+            copies[o, h] = send_image(partial(o, h), o, h)
+        for o, h in ((2, 0), (1, 1)):
+            block = partial(o, h)
+            copies[diagonal, h].wait_recv()
+            copies[o, h] = send_image(block + in_part[diagonal, parts[h], :].astype(F32), o, h)
+        taken = ((1, 0), (2, 1), (2, 0), (1, 1))
+    else:
+        taken = tuple((o, h) for o in range(n_tm - 1, 0, -1) for h in range(2))
+        for o, h in taken:
+            copies[o, h] = send_image(partial(o, h), o, h)
+    for h in range(2):
+        image[parts[h], :] = partial(0, h)
+    for o, h in taken:
+        copies[o, h].wait_recv()
+        image[parts[h], :] += in_part[o, parts[h], :].astype(F32)
     store = pltpu.make_async_copy(image, image_ref, store_sem.at[1])
     store.start()
-    for copy in sent:
+    for copy in list(arrivals.values()) + list(copies.values()):
         copy.wait_send()
     basis_store.wait()
     store.wait()
@@ -204,9 +254,9 @@
             pltpu.VMEM((n_tm, own, k), BF16),
             pltpu.VMEM((n_tm, own, k), BF16),
             pltpu.VMEM((own, k), F32),
-            dma((n_tm,)), dma, dma((n_tm,)), dma((n_tm,)),
+            dma((n_tm,)), dma, dma((n_tm, 2)), dma((n_tm, 2)),
             dma, dma, dma((n_z,)), dma((n_z,)), dma((n_z,)), dma((n_z,)),
-            dma, dma, dma((n_tm,)), dma((n_tm,)), dma((n_tm,)), dma((n_tm,)), dma((2,)),
+            dma, dma, dma((n_tm,)), dma((n_tm,)), dma((n_tm, 2)), dma((n_tm, 2)), dma((2,)),
         ],
         compiler_params=pltpu.CompilerParams(
             collective_id=0, has_side_effects=True, vmem_limit_bytes=48 * 1024 * 1024

time: 78.9 us -> 69.7 us (0.88)
  Pallas kernels: 75.6 us -> 66.4 us
    pallas_call x1, Pallas kernels: 75.6 us -> 66.4 us  [on_device(): pl.pallas_call(functools.partial(kernel, n_panel, n_tm), out_shape=(jax.S...]
where the time goes in v2:
time: 69.7 us; the launch traced here: 69.6 us
  Pallas kernels  66.4 us (95%)
  local copies, waits for them, and re-layouts  2.55 us (4%)
    pallas_call x1, Pallas kernels, on_device(): pl.pallas_call(functools.partial(kernel, n_panel, n_tm), out_shape=(jax.S...  66.4 us
    unnamed x4, local copies, waits for them, and re-layouts  2.55 us

profile of v2, /device:TPU:0, one launch (start us, length us, event | category | flops | bytes accessed | tf_op | source)
XLA Modules:
  0.0 69.6 jit_solution(17480969495991823104)
XLA Ops:
  0.6 0.0 copy-start
  0.6 1.0 %copy-done = bf16[1536,128]{1,0:T(8,128)(2,1)S(1)} copy-done((bf16[1536,128]{1,0:T(8,128)(2,1)S(1)}, bf16[1536,128]{1,0:T(8,128)(2,1)}, u32[]{:S(2)}) %copy-start) | copy-done | bytes 393240
  1.6 66.4 %shard_map.41 = (bf16[768,128]{1,0:T(8,128)(2,1)S(1)}, f32[1536,128]{1,0:T(8,128)S(1)}) custom-call(bf16[6144,768]{1,0:T(8,128)(2,1)} %p_hbm.1, bf16[1536,128]{1,0:T(8,128)(2,1)S(1)} %copy-done), custom_call_target="tpu_custom_call" | custom-call | flops 2415919104 | bytes 9437184 | tf_op jit(solution)/shard_map/pallas_call | solution.py:237
  68.0 0.7 copy.6
  68.7 0.9 %copy.7 = f32[1536,128]{1,0:T(8,128)} copy(f32[1536,128]{1,0:T(8,128)S(1)} %get-tuple-element.5) | data formatting | bytes 1572864
Async XLA Ops:
  0.6 1.0 %copy-start = (bf16[1536,128]{1,0:T(8,128)(2,1)S(1)}, bf16[1536,128]{1,0:T(8,128)(2,1)}, u32[]{:S(2)}) copy-start(bf16[1536,128]{1,0:T(8,128)(2,1)} %s_hbm.1) | copy-start | bytes 1179652
